TPU v7x, 32 devices: a whole 2x2x4 slice. The times are simulated.
32 devices in a mesh: grp: 2 (over x), loop: 16 (over z, y, core).
Axes of the slice: x: 2, y: 2, z: 4, core: 2. Of those that a mesh axis runs over, the one named last changes fastest.
Arguments:
- rows_in: bfloat16 [512, 6144], P(('grp', 'loop')), parts along dimension 0, may hold values from -6 to 6
- rows_grad: bfloat16 [512, 6144], P(('grp', 'loop')), parts along dimension 0, may hold values from -6 to 6
- route_weight: float32 [512, 2], P('grp'), parts along dimension 0, may hold values from 0.1 to 0.9
- expert_ids: int32 [512, 2], P('grp'), parts along dimension 0, may hold values from 0 to 7, all different within a row; in each aligned block of 256 rows (0 to 255, 256 to 511, ...) at most 128 rows name the same one
- w_gate: bfloat16 [6144, 16384], P(None, 'loop'), may hold values from -0.078125 to 0.078125
- w_up: bfloat16 [6144, 16384], P(None, 'loop'), may hold values from -0.078125 to 0.078125
- w_down: bfloat16 [16384, 6144], P('loop'), may hold values from -0.046875 to 0.046875
- delta_in: bfloat16 [2048, 6144], P('loop'), may hold values from -0.078125 to 0.078125
- delta_out: bfloat16 [2048, 6144], P('loop'), may hold values from -0.375 to 0.375
Outputs:
- grad_rows: bfloat16 [512, 6144], P(('grp', 'loop')), parts along dimension 0
- grad_gate: bfloat16 [12288, 16384], P('grp', 'loop'), parts along dimension 0
- grad_up: bfloat16 [12288, 16384], P('grp', 'loop'), parts along dimension 0
- grad_down: bfloat16 [32768, 6144], P(('grp', 'loop')), parts along dimension 0
- grad_delta_in: bfloat16 [4096, 6144], P(('grp', 'loop')), parts along dimension 0
- grad_delta_out: bfloat16 [4096, 6144], P(('grp', 'loop')), parts along dimension 0
There are 2 independent parts, one for each index of `grp`. A program takes and returns all parts, laid end to end along the dimension named above; an argument that names none is the same for every part. Nothing has to cross between parts.
Inputs may be any that keep to these rules, and one draw needn't show every extreme that they name: `expert_ids`: each row names 2 different experts; every expert is named by some row; no expert is named by more than 128 rows, a bound that some block reaches.
All inputs are finite; a program needn't handle non-finite values.
Results may differ from a plain program's by a relative error of at most 0.005.
Values may be sent and summed in bfloat16 or wider, within the bound.
A program may use at most 192 MiB of HBM per device.

v0:
```python
import jax
import jax.numpy as jnp
from jax import lax
from jax.sharding import PartitionSpec as P

RANK = 256


def per_device(
    rows_in, rows_grad, route_weight, expert_ids, w_gate, w_up, w_down, delta_in, delta_out
):
    inputs, cotangent = (
        lax.all_gather(rows_in, "loop", axis=0, tiled=True),
        lax.all_gather(rows_grad, "loop", axis=0, tiled=True),
    )
    gate = jnp.dot(inputs, w_gate, preferred_element_type=jnp.float32)
    up = jnp.dot(inputs, w_up, preferred_element_type=jnp.float32)
    sig = jax.nn.sigmoid(gate)
    hidden = (gate * sig * up).astype(jnp.bfloat16)
    grad_hidden = jnp.dot(cotangent, w_down.T, preferred_element_type=jnp.float32)
    grad_pre_gate = (grad_hidden * up * sig * (1.0 + gate * (1.0 - sig))).astype(jnp.bfloat16)
    grad_pre_up = (grad_hidden * gate * sig).astype(jnp.bfloat16)
    grad_down = jnp.dot(hidden.T, cotangent, preferred_element_type=jnp.float32).astype(
        jnp.bfloat16
    )
    grad_gate = jnp.dot(inputs.T, grad_pre_gate, preferred_element_type=jnp.float32).astype(
        jnp.bfloat16
    )
    grad_up = jnp.dot(inputs.T, grad_pre_up, preferred_element_type=jnp.float32).astype(
        jnp.bfloat16
    )
    owned = delta_in.shape[0]
    expert = lax.axis_index("loop") * owned // RANK
    matched = expert_ids == expert
    coef = jnp.sum(jnp.where(matched, route_weight, jnp.zeros_like(route_weight)), axis=1)
    proj = jnp.dot(inputs, delta_in.T, preferred_element_type=jnp.float32)
    back = jnp.dot(cotangent, delta_out.T, preferred_element_type=jnp.float32)
    grad_z = (coef[:, None] * back).astype(jnp.bfloat16)
    scaled_z = (coef[:, None] * proj).astype(jnp.bfloat16)
    grad_delta_in = jnp.dot(grad_z.T, inputs, preferred_element_type=jnp.float32).astype(
        jnp.bfloat16
    )
    grad_delta_out = jnp.dot(scaled_z.T, cotangent, preferred_element_type=jnp.float32).astype(
        jnp.bfloat16
    )
    delta_rows_term = jnp.dot(grad_z, delta_in, preferred_element_type=jnp.float32)
    partial_value = jnp.dot(grad_pre_gate, w_gate.T, preferred_element_type=jnp.float32)
    partial_value = partial_value + jnp.dot(grad_pre_up, w_up.T, preferred_element_type=jnp.float32)
    partial_value = partial_value + delta_rows_term
    summed = lax.psum_scatter(partial_value, "loop", scatter_dimension=0, tiled=True)
    grad_rows = summed.astype(jnp.bfloat16)
    return (grad_rows, grad_gate, grad_up, grad_down, grad_delta_in, grad_delta_out)


def solution(mesh):
    placed = (
        P(("grp", "loop"), None),
        P(("grp", "loop"), None),
        P("grp", None),
        P("grp", None),
        P(None, "loop"),
        P(None, "loop"),
        P("loop", None),
        P("loop", None),
        P("loop", None),
    )
    return jax.shard_map(
        per_device,
        mesh=mesh,
        in_specs=placed,
        out_specs=(
            P(("grp", "loop"), None),
            P("grp", "loop"),
            P("grp", "loop"),
            P(("grp", "loop"), None),
            P(("grp", "loop"), None),
            P(("grp", "loop"), None),
        ),
        check_vma=False,
    )
```

profile of v0, /device:TPU:0, one launch (start us, length us, event | category | flops | bytes accessed | tf_op | source)
XLA Modules:
  0.0 243.8 jit_solution(13470719475990345624)
XLA Ops:
  7.2 0.0 copy-start
  7.2 0.0 all-gather.5.cloned.1.call-start
  7.2 0.7 all-gather.5.cloned.1.call-update
  7.9 0.0 all-gather.3.cloned.1.call-start
  8.0 0.7 all-gather.3.cloned.1.call-update
  8.7 0.0 reduce-scatter.2.cloned.1.call-start
  8.7 0.7 fusion.4
  9.4 48.8 %all-gather.5.cloned.1.call-done = bf16[256,6144]{1,0:T(8,128)(2,1)} async-done(((bf16[16,6144]{1,0:T(8,128)(2,1)}), bf16[256,6144]{1,0:T(8,128)(2,1)}) %all-gather.5.cloned.1.call-update) | async-done | bytes 3145744 | tf_op jit(solution)/shard_map/all_gather | solution.py:13
  58.2 0.0 copy-start.1
  58.2 9.1 %fusion.6 = f32[256,1024]{1,0:T(8,128)S(1)} fusion(bf16[256,6144]{1,0:T(8,128)(2,1)} %all-gather.5.cloned.1.call-done, bf16[6144,1024]{1,0:T(8,128)(2,1)} %param.14), kind=kOutput, calls=%fused_computation.20 | convolution fusion | flops 3221225472 | bytes 16777216 | tf_op jit(solution)/shard_map/dot_general | solution.py:17
  67.3 0.0 copy-done.1
  67.3 0.0 copy-start.3
  67.3 8.0 %fusion.7 = f32[256,1024]{1,0:T(8,128)} fusion(bf16[256,6144]{1,0:T(8,128)(2,1)S(1)} %copy-done.1, bf16[6144,1024]{1,0:T(8,128)(2,1)} %param.13), kind=kOutput, calls=%fused_computation.21 | convolution fusion | flops 3221225472 | bytes 16777216 | tf_op jit(solution)/shard_map/dot_general | solution.py:16
  75.3 29.3 %all-gather.3.cloned.1.call-done = bf16[256,6144]{1,0:T(8,128)(2,1)} async-done(((bf16[16,6144]{1,0:T(8,128)(2,1)}), bf16[256,6144]{1,0:T(8,128)(2,1)}) %all-gather.3.cloned.1.call-update) | async-done | bytes 3145744 | tf_op jit(solution)/shard_map/all_gather | solution.py:14
  104.6 0.0 copy-done.3
  104.6 10.2 %multiply_convert_fusion.1 = (bf16[256,1024]{1,0:T(8,128)(2,1)}, bf16[256,1024]{1,0:T(8,128)(2,1)S(1)}) fusion(f32[256,1024]{1,0:T(8,128)} %fusion.7, f32[256,1024]{1,0:T(8,128)S(1)} %fusion.6, bf16[256,6144]{1,0:T(8,128)(2,1)} %all-gather.3.cloned.1.call-done, bf16[1024,6144]{1,0:T(8,128)(2,1)} %param.15), kind=kOutput, calls=%fused_computation.12 | convolution fusion | flops 3224633344 | bytes 18874368 | tf_op jit(solution)/shard_map/dot_general | solution.py:20
  114.8 0.0 copy-start.6
  114.8 14.8 %fusion.8 = f32[256,6144]{1,0:T(8,128)} fusion(bf16[256,1024]{1,0:T(8,128)(2,1)S(1)} %get-tuple-element.13, bf16[6144,1024]{1,0:T(8,128)(2,1)} %param.13), kind=kOutput, calls=%fused_computation.22 | convolution fusion | flops 3221225472 | bytes 19398656 | tf_op jit(solution)/shard_map/dot_general | solution.py:47
  129.6 0.0 copy-done.6
  129.6 0.0 copy-start.2
  129.6 12.8 %convolution_add_fusion.1 = f32[256,6144]{1,0:T(8,128)} fusion(f32[256,6144]{1,0:T(8,128)} %fusion.8, bf16[256,1024]{1,0:T(8,128)(2,1)} %get-tuple-element.12, bf16[6144,1024]{1,0:T(8,128)(2,1)} %param.14), kind=kOutput, calls=%fused_computation.4 | convolution fusion | flops 3222798336 | bytes 25690112 | tf_op jit(solution)/shard_map/dot_general | solution.py:48
  142.5 0.0 copy-done.2
  142.5 2.5 %fusion = bf16[256,128]{1,0:T(8,128)(2,1)S(1)} fusion(bf16[256,6144]{1,0:T(8,128)(2,1)S(1)} %copy-done.2, bf16[128,6144]{1,0:T(8,128)(2,1)} %param.17, f32[256]{0:T(256)S(1)} %fusion.4), kind=kOutput, calls=%fused_computation.9 | convolution fusion | flops 402718720 | bytes 4785152 | tf_op jit(solution)/shard_map/dot_general | solution.py:37
  145.0 0.0 copy-done
  145.0 6.4 %convolution_add_fusion = f32[256,6144]{1,0:T(8,128)} fusion(f32[256,6144]{1,0:T(8,128)} %convolution_add_fusion.1, bf16[256,128]{1,0:T(8,128)(2,1)S(1)} %fusion, bf16[128,6144]{1,0:T(8,128)(2,1)S(1)} %copy-done), kind=kOutput, calls=%fused_computation.3 | convolution fusion | flops 404226048 | bytes 14221312 | tf_op jit(solution)/shard_map/dot_general | solution.py:46
  151.4 0.0 copy-start.7
  151.4 0.0 reduce-scatter.2.cloned.1.call-update
  151.4 1.0 copy-done.7
  152.4 8.7 %convert_bitcast_fusion.1 = bf16[6144,1024]{0,1:T(8,128)(2,1)} fusion(bf16[256,1024]{1,0:T(8,128)(2,1)S(1)} %copy-done.7, bf16[256,6144]{1,0:T(8,128)(2,1)} %all-gather.5.cloned.1.call-done), kind=kOutput, calls=%fused_computation.1 | convolution fusion | flops 3227516928 | bytes 16252928 | tf_op jit(solution)/shard_map/dot_general | solution.py:26
  161.1 0.0 copy-start.5
  161.1 17.0 %copy.15 = bf16[6144,1024]{1,0:T(8,128)(2,1)} copy(bf16[6144,1024]{0,1:T(8,128)(2,1)} %convert_bitcast_fusion.1) | data formatting | bytes 25165824
  178.1 0.0 copy-done.5
  178.1 8.5 %convert_bitcast_fusion = bf16[6144,1024]{0,1:T(8,128)(2,1)} fusion(bf16[256,1024]{1,0:T(8,128)(2,1)S(1)} %copy-done.5, bf16[256,6144]{1,0:T(8,128)(2,1)} %all-gather.5.cloned.1.call-done), kind=kOutput, calls=%fused_computation | convolution fusion | flops 3227516928 | bytes 16252928 | tf_op jit(solution)/shard_map/dot_general | solution.py:29
  186.6 16.6 %copy.16 = bf16[6144,1024]{1,0:T(8,128)(2,1)} copy(bf16[6144,1024]{0,1:T(8,128)(2,1)} %convert_bitcast_fusion) | data formatting | bytes 25165824
  203.3 3.7 %convolution_convert_fusion.2 = bf16[128,6144]{1,0:T(8,128)(2,1)} fusion(bf16[256,128]{1,0:T(8,128)(2,1)S(1)} %fusion, bf16[256,6144]{1,0:T(8,128)(2,1)} %all-gather.5.cloned.1.call-done), kind=kOutput, calls=%fused_computation.6 | convolution fusion | flops 403439616 | bytes 4784128 | tf_op jit(solution)/shard_map/dot_general | solution.py:40
  206.9 0.0 copy-start.4
  206.9 6.5 %convolution_convert_fusion.1 = bf16[128,6144]{1,0:T(8,128)(2,1)} fusion(bf16[256,6144]{1,0:T(8,128)(2,1)} %all-gather.3.cloned.1.call-done, bf16[256,6144]{1,0:T(8,128)(2,1)} %all-gather.5.cloned.1.call-done, bf16[128,6144]{1,0:T(8,128)(2,1)S(1)} %copy-done, f32[256]{0:T(256)S(1)} %fusion.4), kind=kOutput, calls=%fused_computation.5 | convolution fusion | flops 806158336 | bytes 9438208 | tf_op jit(solution)/shard_map/dot_general | solution.py:43
  213.4 0.0 copy-done.4
  213.4 10.6 %convolution_convert_fusion = bf16[1024,6144]{1,0:T(8,128)(2,1)} fusion(bf16[256,6144]{1,0:T(8,128)(2,1)} %all-gather.3.cloned.1.call-done, f32[256,1024]{1,0:T(8,128)S(1)} %copy-done.4, f32[256,1024]{1,0:T(8,128)} %fusion.7), kind=kOutput, calls=%fused_computation.2 | convolution fusion | flops 3229089792 | bytes 17825792 | tf_op jit(solution)/shard_map/dot_general | solution.py:23
  224.0 11.6 %reduce-scatter.2.cloned.1.call-done = f32[16,6144]{1,0:T(8,128)} async-done(((f32[256,6144]{1,0:T(8,128)}), f32[16,6144]{1,0:T(8,128)}) %reduce-scatter.2.cloned.1.call-update) | async-done | bytes 393232 | tf_op jit(solution)/shard_map/reduce_scatter | solution.py:50
  235.6 1.7 convert_element_type.42
Async XLA Ops:
  7.2 137.8 %copy-start = (bf16[128,6144]{1,0:T(8,128)(2,1)S(1)}, bf16[128,6144]{1,0:T(8,128)(2,1)}, u32[]{:S(2)}) copy-start(bf16[128,6144]{1,0:T(8,128)(2,1)} %param.16) | copy-start | bytes 4718596
  7.2 51.0 %all-gather.5.cloned.1.call-start = ((), (), s32[]{:S(2)}) async-start(), calls=%async_computation.2 | async-start | bytes 3342336 | tf_op jit(solution)/shard_map/all_gather | solution.py:13
  7.9 96.7 %all-gather.3.cloned.1.call-start = ((), (), s32[]{:S(2)}) async-start(), calls=%async_computation.1 | async-start | bytes 3342336 | tf_op jit(solution)/shard_map/all_gather | solution.py:14
  8.7 226.9 %reduce-scatter.2.cloned.1.call-start = ((), (), s32[]{:S(2)}) async-start(), calls=%async_computation.3 | async-start | bytes 6684672 | tf_op jit(solution)/shard_map/reduce_scatter | solution.py:50
  58.2 9.1 %copy-start.1 = (bf16[256,6144]{1,0:T(8,128)(2,1)S(1)}, bf16[256,6144]{1,0:T(8,128)(2,1)}, u32[]{:S(2)}) copy-start(bf16[256,6144]{1,0:T(8,128)(2,1)} %all-gather.5.cloned.1.call-done) | copy-start | bytes 9437188
  67.3 37.3 %copy-start.3 = (f32[256,1024]{1,0:T(8,128)}, f32[256,1024]{1,0:T(8,128)S(1)}, u32[]{:S(2)}) copy-start(f32[256,1024]{1,0:T(8,128)S(1)} %fusion.6) | copy-start | bytes 3145732
  114.8 14.8 %copy-start.6 = (bf16[256,1024]{1,0:T(8,128)(2,1)}, bf16[256,1024]{1,0:T(8,128)(2,1)S(1)}, u32[]{:S(2)}) copy-start(bf16[256,1024]{1,0:T(8,128)(2,1)S(1)} %get-tuple-element.13) | copy-start | bytes 1572868
  129.6 12.8 %copy-start.2 = (bf16[256,6144]{1,0:T(8,128)(2,1)S(1)}, bf16[256,6144]{1,0:T(8,128)(2,1)}, u32[]{:S(2)}) copy-start(bf16[256,6144]{1,0:T(8,128)(2,1)} %all-gather.3.cloned.1.call-done) | copy-start | bytes 9437188
  151.4 1.0 copy-start.7
  161.1 17.0 %copy-start.5 = (bf16[256,1024]{1,0:T(8,128)(2,1)S(1)}, bf16[256,1024]{1,0:T(8,128)(2,1)}, u32[]{:S(2)}) copy-start(bf16[256,1024]{1,0:T(8,128)(2,1)} %get-tuple-element.12) | copy-start | bytes 1572868
  206.9 6.5 %copy-start.4 = (f32[256,1024]{1,0:T(8,128)S(1)}, f32[256,1024]{1,0:T(8,128)}, u32[]{:S(2)}) copy-start(f32[256,1024]{1,0:T(8,128)} %copy-done.3) | copy-start | bytes 3145732
Sparse Core Ops, SparseCore 0:
  10.3 47.8 all-gather.4
  60.5 44.0 all-gather.2
  151.5 84.0 reduce-scatter.1
where the time goes:
time: 245 us; the launch traced here: 244 us
  matrix products  102 us (42%)
  waiting for transfers between devices  91.1 us (37%)
  local copies, waits for them, and re-layouts  34.7 us (14%)
  between operations  13.8 us (6%)
    all_gather x1, waiting for transfers between devices, per_device(): lax.all_gather(rows_in, 'loop', axis=0, tiled=True)  48.8 us
    unnamed x18, local copies, waits for them, and re-layouts  34.7 us
    all_gather x1, waiting for transfers between devices, per_device(): lax.all_gather(rows_grad, 'loop', axis=0, tiled=True)  29.3 us
    dot_general x1, matrix products, per_device(): jnp.dot(grad_pre_gate, w_gate.T, preferred_element_type=jnp.float32)  14.8 us
    dot_general x1, matrix products, per_device(): jnp.dot(grad_pre_up, w_up.T, preferred_element_type=jnp.float32)  12.8 us
    reduce_scatter x1, waiting for transfers between devices, per_device(): lax.psum_scatter(partial_value, 'loop', scatter_dimension=0, tiled=True)  11.6 us
    dot_general x1, matrix products, per_device(): jnp.dot(hidden.T, cotangent, preferred_element_type=jnp.float32)  10.6 us
    dot_general x1, matrix products, per_device(): jnp.dot(cotangent, w_down.T, preferred_element_type=jnp.float32)  10.2 us
  transfers between devices with their start and end apart: 3, of which 3 were waited for; matrix products, arithmetic and copies ran while one was open for 37% of the time, Pallas kernels for 0%

commit v1 on v0

--- a/solution.py
+++ b/solution.py
@@ -1,9 +1,329 @@
+import functools
+
 import jax
 import jax.numpy as jnp
 from jax import lax
+from jax.experimental import pallas as pl
+from jax.experimental.pallas import tpu as pltpu
 from jax.sharding import PartitionSpec as P
 
 RANK = 256
+BF = jnp.bfloat16
+F32 = jnp.float32
+MESH = pl.DeviceIdType.MESH
+NT = (((1,), (1,)), ((), ()))
+TN = (((0,), (0,)), ((), ()))
+
+
+def dot_nt(a, b):
+    return lax.dot_general(a, b, NT, preferred_element_type=F32)
+
+
+def dot_tn(a, b):
+    return lax.dot_general(a, b, TN, preferred_element_type=F32)
+
+
+def forward_kernel(
+    chunks,
+    rows_in, rows_grad, coef, w_gate, w_up, w_down, delta_in, delta_out,
+    grad_rows, x_out, g_out, hid_out, gpg_out, gpu_out, dz_out, cz_out,
+    act, wg, wu, wd, din, dout, fac_a, fac_b, hid, gpg, gpu, dz, cz,
+    part, c_in, c_sum, y_in, y_sum, z_in,
+    load_sem, own_sem, out_sem, send_sem, recv_sem,
+    c_send, c_recv, y_send, y_recv, z_send, z_recv,
+):
+    me = lax.axis_index("loop")
+    z, y, c = me // 4, (me // 2) % 2, me % 2
+    rows = rows_in.shape[0]
+    tile = 256
+    width = part.shape[-1]
+
+    def zpeer(d):
+        return ((z // 2 + d // 2) % 2) * 2 + (z % 2 + d % 2) % 2
+
+    def ident(zz, yy, cc):
+        return zz * 4 + yy * 2 + cc
+
+    loads = [
+        pltpu.make_async_copy(w_gate, wg, load_sem.at[0]),
+        pltpu.make_async_copy(w_up, wu, load_sem.at[1]),
+        pltpu.make_async_copy(delta_in, din, load_sem.at[2]),
+        pltpu.make_async_copy(w_down, wd, load_sem.at[3]),
+        pltpu.make_async_copy(delta_out, dout, load_sem.at[4]),
+    ]
+    own = [
+        pltpu.make_async_copy(src, act.at[a, pl.ds(me * rows, rows)], own_sem.at[a])
+        for a, src in enumerate((rows_in, rows_grad))
+    ]
+    for cp in own + loads:
+        cp.start()
+
+    barrier = pltpu.get_barrier_semaphore()
+    for d in range(1, 4):
+        pl.semaphore_signal(
+            barrier, inc=1, device_id={"loop": ident(zpeer(d), y, c)}, device_id_type=MESH
+        )
+    pl.semaphore_signal(barrier, inc=1, device_id={"loop": ident(z, 1 - y, c)}, device_id_type=MESH)
+    pl.semaphore_signal(barrier, inc=1, device_id={"loop": ident(z, y, 1 - c)}, device_id_type=MESH)
+    pl.semaphore_wait(barrier, 5)
+
+    def block_copy(a, block, target, slot):
+        ref = act.at[a, pl.ds(block * rows, rows)]
+        return pltpu.make_async_remote_copy(
+            src_ref=ref, dst_ref=ref, send_sem=send_sem.at[a, slot], recv_sem=recv_sem.at[a, block],
+            device_id={"loop": target}, device_id_type=MESH,
+        )
+
+    def to_z(a, d):
+        return block_copy(a, me, ident(zpeer(d), y, c), d - 1)
+
+    def to_y(a, d):
+        return block_copy(a, ident(zpeer(d), y, c), ident(z, 1 - y, c), 3 + d)
+
+    def to_core(a, d, yy, slot):
+        return block_copy(a, ident(zpeer(d), yy, c), ident(z, y, 1 - c), slot)
+
+    def arrived(a, block):
+        block_copy(a, block, me + 1 - 2 * c, 0).wait_recv()
+
+    for a in range(2):
+        own[a].wait()
+        to_y(a, 0).start()
+        for d in range(1, 4):
+            to_z(a, d).start()
+        to_core(a, 0, y, 7).start()
+
+    def relay(a, j):
+        @pl.when(j < 3)
+        def _():
+            arrived(a, ident(zpeer(j + 1), y, c))
+            to_y(a, j + 1).start()
+            to_core(a, j + 1, y, 8 + j).start()
+
+        arrived(a, ident(zpeer(j), 1 - y, c))
+        to_core(a, j, 1 - y, 11 + j).start()
+
+    def settle(a):
+        @pl.loop(0, 4)
+        def _(j):
+            arrived(a, ident(zpeer(j), y, 1 - c))
+            arrived(a, ident(zpeer(j), 1 - y, 1 - c))
+
+    @pl.loop(0, 4)
+    def _(j):
+        relay(0, j)
+
+    settle(0)
+    x_copy = pltpu.make_async_copy(act.at[0], x_out, out_sem.at[0])
+    x_copy.start()
+    loads[0].wait()
+    loads[1].wait()
+    loads[2].wait()
+
+    n_tiles = hid.shape[1] // tile
+
+    @pl.loop(0, n_tiles)
+    def _(j):
+        cols = pl.ds(pl.multiple_of(j * tile, tile), tile)
+        gate = jnp.dot(act[0], wg[:, cols], preferred_element_type=F32)
+        up = jnp.dot(act[0], wu[:, cols], preferred_element_type=F32)
+        sig = jax.nn.sigmoid(gate)
+        silu = gate * sig
+        hid[:, cols] = (silu * up).astype(BF)
+        fac_b[:, cols] = silu
+        fac_a[:, cols] = up * sig * (1.0 + gate * (1.0 - sig))
+
+        @pl.when(j < 4)
+        def _():
+            relay(1, j)
+
+    proj = dot_nt(act[0], din[...])
+    cz[...] = (coef[...] * proj).astype(BF)
+    settle(1)
+    g_copy = pltpu.make_async_copy(act.at[1], g_out, out_sem.at[1])
+    g_copy.start()
+    loads[3].wait()
+    loads[4].wait()
+    back = dot_nt(act[1], dout[...])
+    dz[...] = (coef[...] * back).astype(BF)
+
+    @pl.loop(0, n_tiles)
+    def _(j):
+        cols = pl.ds(pl.multiple_of(j * tile, tile), tile)
+        grad_hidden = dot_nt(act[1], wd[cols, :])
+        gpg[:, cols] = (grad_hidden * fac_a[:, cols]).astype(BF)
+        gpu[:, cols] = (grad_hidden * fac_b[:, cols]).astype(BF)
+
+    outs = [
+        pltpu.make_async_copy(src, dst, out_sem.at[2 + i])
+        for i, (src, dst) in enumerate(
+            ((hid, hid_out), (gpg, gpg_out), (gpu, gpu_out), (dz, dz_out), (cz, cz_out))
+        )
+    ]
+    for cp in outs:
+        cp.start()
+
+    def c_copy(s):
+        return pltpu.make_async_remote_copy(
+            src_ref=part.at[s, :, 1 - c], dst_ref=c_in.at[s], send_sem=c_send.at[s],
+            recv_sem=c_recv.at[s], device_id={"loop": ident(z, y, 1 - c)}, device_id_type=MESH,
+        )
+
+    def y_copy(s):
+        return pltpu.make_async_remote_copy(
+            src_ref=c_sum.at[s, :, 1 - y], dst_ref=y_in.at[s], send_sem=y_send.at[s],
+            recv_sem=y_recv.at[s], device_id={"loop": ident(z, 1 - y, c)}, device_id_type=MESH,
+        )
+
+    def z_copy(s, d):
+        return pltpu.make_async_remote_copy(
+            src_ref=y_sum.at[s, zpeer(d)], dst_ref=z_in.at[s, d - 1], send_sem=z_send.at[s, d - 1],
+            recv_sem=z_recv.at[s, d - 1], device_id={"loop": ident(zpeer(d), y, c)},
+            device_id_type=MESH,
+        )
+
+    @pl.loop(0, chunks + 3)
+    def _(s):
+        @pl.when(s < chunks)
+        def _():
+            cols = pl.ds(pl.multiple_of(s * width, width), width)
+            total = dot_nt(gpg[...], wg[cols, :]) + dot_nt(gpu[...], wu[cols, :])
+            total = total + jnp.dot(dz[...], din[:, cols], preferred_element_type=F32)
+            part[s] = total.astype(BF).reshape(part.shape[1:])
+            c_copy(s).start()
+
+        @pl.when((s >= 1) & (s < chunks + 1))
+        def _():
+            t = s - 1
+            c_copy(t).wait_recv()
+            add = part[t, :, c].astype(F32) + c_in[t].astype(F32)
+            c_sum[t] = add.astype(BF).reshape(c_sum.shape[1:])
+            y_copy(t).start()
+
+        @pl.when((s >= 2) & (s < chunks + 2))
+        def _():
+            t = s - 2
+            y_copy(t).wait_recv()
+            y_sum[t] = (c_sum[t, :, y].astype(F32) + y_in[t].astype(F32)).astype(BF)
+            for d in range(1, 4):
+                z_copy(t, d).start()
+
+        @pl.when(s >= 3)
+        def _():
+            t = s - 3
+            total = y_sum[t, z].astype(F32)
+            for d in range(1, 4):
+                z_copy(t, d).wait_recv()
+                total = total + z_in[t, d - 1].astype(F32)
+            cols = pl.ds(pl.multiple_of(t * width, width), width)
+            grad_rows[:, cols] = total.astype(BF)
+
+    @pl.loop(0, chunks)
+    def _(s):
+        c_copy(s).wait_send()
+        y_copy(s).wait_send()
+        for d in range(1, 4):
+            z_copy(s, d).wait_send()
+
+    for a in range(2):
+        for slot in range(15):
+            block_copy(a, me, me + 1 - 2 * c, slot).wait_send()
+    x_copy.wait()
+    g_copy.wait()
+    for cp in outs:
+        cp.wait()
+
+
+def forward(rows_in, rows_grad, coef, w_gate, w_up, w_down, delta_in, delta_out):
+    rows, d = rows_in.shape
+    tokens = rows * 16
+    ff = w_gate.shape[1]
+    own = delta_in.shape[0]
+    width = 1024
+    chunks = d // width
+    sds = jax.ShapeDtypeStruct
+    dma = pltpu.SemaphoreType.DMA
+    vmem = pltpu.VMEM
+    hbm = pl.BlockSpec(memory_space=pl.ANY)
+    return pl.pallas_call(
+        functools.partial(forward_kernel, chunks),
+        out_shape=(
+            sds((rows, d), BF), sds((tokens, d), BF), sds((tokens, d), BF),
+            sds((tokens, ff), BF), sds((tokens, ff), BF), sds((tokens, ff), BF),
+            sds((tokens, own), BF), sds((tokens, own), BF),
+        ),
+        in_specs=[hbm, hbm, pl.BlockSpec(memory_space=pltpu.VMEM)] + [hbm] * 5,
+        out_specs=[pl.BlockSpec(memory_space=pltpu.VMEM)] + [hbm] * 7,
+        scratch_shapes=[
+            vmem((2, tokens, d), BF), vmem((d, ff), BF), vmem((d, ff), BF), vmem((ff, d), BF),
+            vmem((own, d), BF), vmem((own, d), BF),
+            vmem((tokens, ff), F32), vmem((tokens, ff), F32),
+            vmem((tokens, ff), BF), vmem((tokens, ff), BF), vmem((tokens, ff), BF),
+            vmem((tokens, own), BF), vmem((tokens, own), BF),
+            vmem((chunks, 8, 2, rows, width), BF), vmem((chunks, 8, rows, width), BF),
+            vmem((chunks, 4, 2, rows, width), BF), vmem((chunks, 4, rows, width), BF),
+            vmem((chunks, 4, rows, width), BF), vmem((chunks, 3, rows, width), BF),
+            dma((5,)), dma((2,)), dma((7,)), dma((2, 15)), dma((2, 16)),
+            dma((chunks,)), dma((chunks,)), dma((chunks,)), dma((chunks,)),
+            dma((chunks, 3)), dma((chunks, 3)),
+        ],
+        compiler_params=pltpu.CompilerParams(
+            collective_id=0, has_side_effects=True, vmem_limit_bytes=63 * 1024 * 1024
+        ),
+        cost_estimate=pl.CostEstimate(
+            flops=2 * tokens * d * (5 * ff + 3 * own), bytes_accessed=2 * d * (3 * ff + 3 * tokens),
+            transcendentals=tokens * ff,
+        ),
+    )(rows_in, rows_grad, coef, w_gate, w_up, w_down, delta_in, delta_out)
+
+
+def weight_kernel(x, g, hid, gpg, gpu, dz, cz, o_gate, o_up, o_down, o_in, o_out):
+    xt = x[...].T
+    o_gate[...] = jnp.dot(xt, gpg[...], preferred_element_type=F32).astype(BF)
+    o_up[...] = jnp.dot(xt, gpu[...], preferred_element_type=F32).astype(BF)
+    o_down[...] = dot_tn(hid[...], g[...]).astype(BF)
+    o_in[...] = dot_tn(dz[...], x[...]).astype(BF)
+    o_out[...] = dot_tn(cz[...], g[...]).astype(BF)
+
+
+def weight_grads(x, g, hid, gpg, gpu, dz, cz):
+    tokens, d = x.shape
+    ff, own = hid.shape[1], dz.shape[1]
+    step = 512
+    sds = jax.ShapeDtypeStruct
+    full = lambda n: pl.BlockSpec((tokens, n), lambda i: (0, 0))
+    part = pl.BlockSpec((tokens, step), lambda i: (0, i))
+    tall = pl.BlockSpec((step, ff), lambda i: (i, 0))
+    return pl.pallas_call(
+        weight_kernel,
+        grid=(d // step,),
+        out_shape=(sds((d, ff), BF), sds((d, ff), BF), sds((ff, d), BF), sds((own, d), BF), sds((own, d), BF)),
+        in_specs=[part, part, full(ff), full(ff), full(ff), full(own), full(own)],
+        out_specs=[tall, tall] + [pl.BlockSpec((n, step), lambda i: (0, i)) for n in (ff, own, own)],
+        compiler_params=pltpu.CompilerParams(vmem_limit_bytes=56 * 1024 * 1024),
+        cost_estimate=pl.CostEstimate(
+            flops=2 * tokens * d * (3 * ff + 2 * own), bytes_accessed=2 * d * (3 * ff + 2 * own + 2 * tokens),
+            transcendentals=0,
+        ),
+    )(x, g, hid, gpg, gpu, dz, cz)
+
+
+def coef_of(route_weight, expert_ids, owned):
+    expert = lax.axis_index("loop") * owned // RANK
+    matched = expert_ids == expert
+    return jnp.sum(jnp.where(matched, route_weight, jnp.zeros_like(route_weight)), axis=1)
+
+
+def fused_device(
+    rows_in, rows_grad, route_weight, expert_ids, w_gate, w_up, w_down, delta_in, delta_out
+):
+    owned = delta_in.shape[0]
+    coef = coef_of(route_weight, expert_ids, owned)
+    coef = jnp.broadcast_to(coef[:, None], (coef.shape[0], owned))
+    grad_rows, x, g, hid, gpg, gpu, dz, cz = forward(
+        rows_in, rows_grad, coef, w_gate, w_up, w_down, delta_in, delta_out
+    )
+    return (grad_rows,) + tuple(weight_grads(x, g, hid, gpg, gpu, dz, cz))
 
 
 def per_device(
@@ -64,8 +384,9 @@
         P("loop", None),
         P("loop", None),
     )
+    device = fused_device if mesh.shape["loop"] == 16 else per_device
     return jax.shard_map(
-        per_device,
+        device,
         mesh=mesh,
         in_specs=placed,
         out_specs=(

time: 245 us -> 119 us (0.49)
  Pallas kernels: 0 us -> 116 us
  matrix products: 102 us -> 0 us
  waiting for transfers between devices: 91.1 us -> 0 us
  local copies, waits for them, and re-layouts: 34.7 us -> 1.44 us
  between operations: 13.8 us -> 0.67 us
    pallas_call x0 -> x2, Pallas kernels: none -> 116 us  [the longest x1 98.1 us: forward(): pl.pallas_call(functools.partial(forward_kernel, chunks), out_shape=(sds(...]
    dot_general x12 -> x0, matrix products: 102 us -> none  [the longest x1 14.8 us: per_device(): jnp.dot(grad_pre_gate, w_gate.T, preferred_element_type=jnp.float32)]
    all_gather x2 -> x0, waiting for transfers between devices: 78.1 us -> none  [the longest x1 48.8 us: per_device(): lax.all_gather(rows_in, 'loop', axis=0, tiled=True)]
    unnamed x18 -> x3, local copies, waits for them, and re-layouts: 34.7 us -> 0.68 us
    reduce_scatter x1 -> x0, waiting for transfers between devices: 11.6 us -> none  [per_device(): lax.psum_scatter(partial_value, 'loop', scatter_dimension=0, tiled=True)]
  transfers between devices with their start and end apart: 3 -> 0, of which waited for: 3 -> 0; matrix products, arithmetic and copies ran while one was open for 37% -> 0% of each run, Pallas kernels for 0% -> 0%
where the time goes in v1:
time: 119 us
  Pallas kernels  116 us (97%)
  local copies, waits for them, and re-layouts  1.44 us (1%)
    pallas_call x1, Pallas kernels, forward(): pl.pallas_call(functools.partial(forward_kernel, chunks), out_shape=(sds(...  98.1 us
    pallas_call x1, Pallas kernels, weight_grads(): pl.pallas_call(weight_kernel, grid=(d // step,), out_shape=(sds((d, ff),...  18 us

profile of v1, /device:TPU:0, one launch (start us, length us, event | category | flops | bytes accessed | tf_op | source)
XLA Modules:
  0.0 118.9 jit_solution(15005013618718620024)
XLA Ops:
  0.6 0.7 fusion
  1.4 0.8 broadcast_in_dim.10.coef
  2.1 98.1 %shard_map.136 = (bf16[16,6144]{1,0:T(8,128)(2,1)}, bf16[256,6144]{1,0:T(8,128)(2,1)}, bf16[256,6144]{1,0:T(8,128)(2,1)}, bf16[256,1024]{1,0:T(8,128)(2,1)}, bf1...) custom-call(bf16[16,6144]{1,0:T(8,128)(2,1)} %rows_in.1, ...), custom_call_target="tpu_custom_call" | custom-call | flops 17314086912 | bytes 47185920 | tf_op jit(solution)/shard_map/pallas_call | solution.py:248
  100.3 0.0 copy-start
  100.3 18.0 %shard_map.137 = (bf16[6144,1024]{1,0:T(8,128)(2,1)}, bf16[6144,1024]{1,0:T(8,128)(2,1)}, bf16[1024,6144]{1,0:T(8,128)(2,1)}, bf16[128,6144]{1,0:T(8,128)(2,1)}, bf16[128,6144]{1,0:T(8,128)(2,1)}) custom-call(bf16[256,6144]{1,0:T(8,128)(2,1)} %get-tuple-element.20.x, bf16[256,6144]{1,0:T(8,128)(2,1)} %get-tuple-element.21.g, ...), custom_call_target="tpu_custom_call" | custom-call | flops 10468982784 | bytes 47185920 | tf_op jit(solution)/shard_map/pallas_call | solution.py:297
  118.2 0.0 copy-done
  118.2 0.7 copy.16
Async XLA Ops:
  100.3 18.0 %copy-start = (bf16[16,6144]{1,0:T(8,128)(2,1)S(1)}, bf16[16,6144]{1,0:T(8,128)(2,1)}, u32[]{:S(2)}) copy-start(bf16[16,6144]{1,0:T(8,128)(2,1)} %get-tuple-element.38) | copy-start | bytes 589828

commit v2 on v1

--- a/solution.py
+++ b/solution.py
@@ -25,7 +25,7 @@
 
 def forward_kernel(
     chunks,
-    rows_in, rows_grad, coef, w_gate, w_up, w_down, delta_in, delta_out,
+    rows_in, rows_grad, route_weight, expert_ids, w_gate, w_up, w_down, delta_in, delta_out,
     grad_rows, x_out, g_out, hid_out, gpg_out, gpu_out, dz_out, cz_out,
     act, wg, wu, wd, din, dout, fac_a, fac_b, hid, gpg, gpu, dz, cz,
     part, c_in, c_sum, y_in, y_sum, z_in,
@@ -137,15 +137,17 @@
         def _():
             relay(1, j)
 
+    matched = expert_ids[...] == me * din.shape[0] // RANK
+    coef = jnp.sum(jnp.where(matched, route_weight[...], 0.0), axis=1, keepdims=True)
     proj = dot_nt(act[0], din[...])
-    cz[...] = (coef[...] * proj).astype(BF)
+    cz[...] = (coef * proj).astype(BF)
     settle(1)
     g_copy = pltpu.make_async_copy(act.at[1], g_out, out_sem.at[1])
     g_copy.start()
     loads[3].wait()
     loads[4].wait()
     back = dot_nt(act[1], dout[...])
-    dz[...] = (coef[...] * back).astype(BF)
+    dz[...] = (coef * back).astype(BF)
 
     @pl.loop(0, n_tiles)
     def _(j):
@@ -234,7 +236,7 @@
         cp.wait()
 
 
-def forward(rows_in, rows_grad, coef, w_gate, w_up, w_down, delta_in, delta_out):
+def forward(rows_in, rows_grad, route_weight, expert_ids, w_gate, w_up, w_down, delta_in, delta_out):
     rows, d = rows_in.shape
     tokens = rows * 16
     ff = w_gate.shape[1]
@@ -252,7 +254,7 @@
             sds((tokens, ff), BF), sds((tokens, ff), BF), sds((tokens, ff), BF),
             sds((tokens, own), BF), sds((tokens, own), BF),
         ),
-        in_specs=[hbm, hbm, pl.BlockSpec(memory_space=pltpu.VMEM)] + [hbm] * 5,
+        in_specs=[hbm] * 2 + [pl.BlockSpec(memory_space=pltpu.VMEM)] * 2 + [hbm] * 5,
         out_specs=[pl.BlockSpec(memory_space=pltpu.VMEM)] + [hbm] * 7,
         scratch_shapes=[
             vmem((2, tokens, d), BF), vmem((d, ff), BF), vmem((d, ff), BF), vmem((ff, d), BF),
@@ -274,13 +276,12 @@
             flops=2 * tokens * d * (5 * ff + 3 * own), bytes_accessed=2 * d * (3 * ff + 3 * tokens),
             transcendentals=tokens * ff,
         ),
-    )(rows_in, rows_grad, coef, w_gate, w_up, w_down, delta_in, delta_out)
+    )(rows_in, rows_grad, route_weight, expert_ids, w_gate, w_up, w_down, delta_in, delta_out)
 
 
 def weight_kernel(x, g, hid, gpg, gpu, dz, cz, o_gate, o_up, o_down, o_in, o_out):
-    xt = x[...].T
-    o_gate[...] = jnp.dot(xt, gpg[...], preferred_element_type=F32).astype(BF)
-    o_up[...] = jnp.dot(xt, gpu[...], preferred_element_type=F32).astype(BF)
+    o_gate[...] = dot_tn(x[...], gpg[...]).astype(BF)
+    o_up[...] = dot_tn(x[...], gpu[...]).astype(BF)
     o_down[...] = dot_tn(hid[...], g[...]).astype(BF)
     o_in[...] = dot_tn(dz[...], x[...]).astype(BF)
     o_out[...] = dot_tn(cz[...], g[...]).astype(BF)
@@ -289,7 +290,7 @@
 def weight_grads(x, g, hid, gpg, gpu, dz, cz):
     tokens, d = x.shape
     ff, own = hid.shape[1], dz.shape[1]
-    step = 512
+    step = 1024
     sds = jax.ShapeDtypeStruct
     full = lambda n: pl.BlockSpec((tokens, n), lambda i: (0, 0))
     part = pl.BlockSpec((tokens, step), lambda i: (0, i))
@@ -308,20 +309,11 @@
     )(x, g, hid, gpg, gpu, dz, cz)
 
 
-def coef_of(route_weight, expert_ids, owned):
-    expert = lax.axis_index("loop") * owned // RANK
-    matched = expert_ids == expert
-    return jnp.sum(jnp.where(matched, route_weight, jnp.zeros_like(route_weight)), axis=1)
-
-
 def fused_device(
     rows_in, rows_grad, route_weight, expert_ids, w_gate, w_up, w_down, delta_in, delta_out
 ):
-    owned = delta_in.shape[0]
-    coef = coef_of(route_weight, expert_ids, owned)
-    coef = jnp.broadcast_to(coef[:, None], (coef.shape[0], owned))
     grad_rows, x, g, hid, gpg, gpu, dz, cz = forward(
-        rows_in, rows_grad, coef, w_gate, w_up, w_down, delta_in, delta_out
+        rows_in, rows_grad, route_weight, expert_ids, w_gate, w_up, w_down, delta_in, delta_out
     )
     return (grad_rows,) + tuple(weight_grads(x, g, hid, gpg, gpu, dz, cz))
 

time: 119 us -> 120 us (level)
  local copies, waits for them, and re-layouts: 1.44 us -> 3.63 us
    unnamed x3 -> x5, local copies, waits for them, and re-layouts: 0.68 us -> 3.63 us
where the time goes in v2:
time: 120 us
  Pallas kernels  115 us (96%)
  local copies, waits for them, and re-layouts  3.63 us (3%)
    pallas_call x1, Pallas kernels, forward(): pl.pallas_call(functools.partial(forward_kernel, chunks), out_shape=(sds(...  98.3 us
    pallas_call x1, Pallas kernels, weight_grads(): pl.pallas_call(weight_kernel, grid=(d // step,), out_shape=(sds((d, ff),...  17.1 us
    unnamed x5, local copies, waits for them, and re-layouts  3.63 us

profile of v2, /device:TPU:0, one launch (start us, length us, event | category | flops | bytes accessed | tf_op | source)
XLA Modules:
  0.0 119.6 jit_solution(11098898001095289923)
XLA Ops:
  0.6 1.5 %copy.15.route_weight = f32[256,2]{1,0:T(8,128)} copy(f32[256,2]{0,1:T(2,128)} %param.11) | data formatting | bytes 4096 | tf_op args[2]
  2.1 1.5 %copy.16.expert_ids = s32[256,2]{1,0:T(8,128)} copy(s32[256,2]{0,1:T(2,128)} %param.12) | data formatting | bytes 4096 | tf_op args[3]
  3.6 98.3 %shard_map.136 = (bf16[16,6144]{1,0:T(8,128)(2,1)}, bf16[256,6144]{1,0:T(8,128)(2,1)}, bf16[256,6144]{1,0:T(8,128)(2,1)}, bf16[256,1024]{1,0:T(8,128)(2,1)}, bf1...) custom-call(bf16[16,6144]{1,0:T(8,128)(2,1)} %rows_in.1, ...), custom_call_target="tpu_custom_call" | custom-call | flops 17314086912 | bytes 47185920 | tf_op jit(solution)/shard_map/pallas_call | solution.py:250
  101.9 0.0 copy-start
  101.9 17.1 %shard_map.137 = (bf16[6144,1024]{1,0:T(8,128)(2,1)}, bf16[6144,1024]{1,0:T(8,128)(2,1)}, bf16[1024,6144]{1,0:T(8,128)(2,1)}, bf16[128,6144]{1,0:T(8,128)(2,1)}, bf16[128,6144]{1,0:T(8,128)(2,1)}) custom-call(bf16[256,6144]{1,0:T(8,128)(2,1)} %get-tuple-element.20.x, bf16[256,6144]{1,0:T(8,128)(2,1)} %get-tuple-element.21.g, ...), custom_call_target="tpu_custom_call" | custom-call | flops 10468982784 | bytes 47185920 | tf_op jit(solution)/shard_map/pallas_call | solution.py:298
  118.9 0.0 copy-done
  119.0 0.7 copy.18
Async XLA Ops:
  101.9 17.1 %copy-start = (bf16[16,6144]{1,0:T(8,128)(2,1)S(1)}, bf16[16,6144]{1,0:T(8,128)(2,1)}, u32[]{:S(2)}) copy-start(bf16[16,6144]{1,0:T(8,128)(2,1)} %get-tuple-element.38) | copy-start | bytes 589828
